TPU v7x, 256 devices: a whole 4x4x8 slice. The times are simulated.
256 devices in a mesh: dp: 16 (over x, y_hi, core), vocab: 8 (over z), tensor: 2 (over y_lo).
Axes of the slice: x: 4, y: 4 (y_hi: 2, y_lo: 2; y = y_hi * 2 + y_lo), z: 8, core: 2. Of those that a mesh axis runs over, the one named last changes fastest.
Arguments:
- residual: bfloat16 [1408, 4096], P('dp', 'tensor'), may hold values from -400 to 400
- norm_gain: float32 [4096], P('tensor'), may hold values from 0.1 to 1.9
- gain_dir: float32 [4096], P('tensor'), may hold values from -6 to 6
- head_weight: bfloat16 [4096, 81920], P('tensor', ('dp', 'vocab')), may hold values from -0.8 to 0.8
- head_dir: bfloat16 [4096, 81920], P('tensor', ('dp', 'vocab')), may hold values from -0.25 to 0.25
- sampled: int32 [1408], replicated, may hold values from 0 to 81919
Outputs:
- fisher_head: float32 [4096, 81920], P('tensor', ('dp', 'vocab'))
- fisher_gain: float32 [4096], P('tensor')
All inputs are finite; a program needn't handle non-finite values.
Results may differ from a plain program's by a relative error of at most 0.012.
The roundings to bfloat16 on the way count: a program that leaves them out, or rounds other values in their place, can miss the bound.
Values may be sent and summed in bfloat16 or wider, within the bound.
No kernel may reach another device: no remote copies, remote signals or barrier semaphores. Data moves between devices by JAX's collectives and lax.ppermute only.
A program may use at most 128 MiB of HBM per device.

v0:
```python
import jax
import jax.numpy as jnp
from jax import lax
from jax.sharding import PartitionSpec as P

EPSILON = 1e-06


def local(residual, norm_gain, gain_dir, head_weight, head_dir, sampled):
    full_width = residual.shape[1] * lax.axis_size("tensor")
    entries = residual.astype(jnp.float32)
    squares = lax.psum(jnp.sum(entries * entries, axis=1), "tensor")
    normed = (entries * lax.rsqrt(squares / full_width + EPSILON)[:, None]).astype(jnp.bfloat16)
    gathered = lax.all_gather(normed, "dp", axis=0, tiled=True)
    spread = gathered.astype(jnp.float32)
    hidden = (spread * norm_gain).astype(jnp.bfloat16)
    tangent = (spread * gain_dir).astype(jnp.bfloat16)
    logits = jnp.dot(hidden, head_weight, preferred_element_type=jnp.float32)
    tangent_logits = jnp.dot(hidden, head_dir, preferred_element_type=jnp.float32) + jnp.dot(
        tangent, head_weight, preferred_element_type=jnp.float32
    )
    logits, tangent_logits = (
        lax.psum_scatter(logits, "tensor", scatter_dimension=0, tiled=True),
        lax.psum_scatter(tangent_logits, "tensor", scatter_dimension=0, tiled=True),
    )
    share_rows = logits.shape[0]
    picked_ids = lax.dynamic_slice_in_dim(
        sampled, lax.axis_index("tensor") * share_rows, share_rows
    )
    vocab_dev = head_weight.shape[1]
    offset = (lax.axis_index("dp") * lax.axis_size("vocab") + lax.axis_index("vocab")) * vocab_dev
    is_picked = lax.broadcasted_iota(jnp.int32, logits.shape, 1) == (picked_ids - offset)[:, None]
    picked_part = jnp.sum(jnp.where(is_picked, tangent_logits, 0.0), axis=1)
    row_top = lax.pmax(jnp.max(logits, axis=1), ("dp", "vocab"))
    scaled_exp = jnp.exp(logits - row_top[:, None])
    row_total, weighted, picked = lax.psum(
        (jnp.sum(scaled_exp, axis=1), jnp.sum(scaled_exp * tangent_logits, axis=1), picked_part),
        ("dp", "vocab"),
    )
    row_probs = scaled_exp / row_total[:, None]
    row_score = picked - weighted / row_total
    cotangent = (row_score[:, None] * (is_picked.astype(jnp.float32) - row_probs)).astype(
        jnp.bfloat16
    )
    full_cot = lax.all_gather(cotangent, "tensor", axis=0, tiled=True)
    product = lax.dot_general(
        gathered, full_cot, (((0,), (0,)), ((), ())), preferred_element_type=jnp.float32
    )
    fisher_head = norm_gain[:, None] * product
    fisher_gain = lax.psum(
        jnp.sum(head_weight.astype(jnp.float32) * product, axis=1), ("dp", "vocab")
    )
    return (fisher_head, fisher_gain)


def solution(mesh):
    in_specs = (
        P("dp", "tensor"),
        P("tensor"),
        P("tensor"),
        P("tensor", ("dp", "vocab")),
        P("tensor", ("dp", "vocab")),
        P(),
    )
    out_specs = (P("tensor", ("dp", "vocab")), P("tensor"))
    return jax.shard_map(local, mesh=mesh, in_specs=in_specs, out_specs=out_specs, check_vma=False)
```

profile of v0, /device:TPU:8, one launch (start us, length us, event | category | flops | bytes accessed | tf_op | source)
XLA Modules:
  0.0 1515.0 jit_solution(15969742382134527424)
XLA Ops:
  7.2 0.0 copy-start
  7.2 0.0 all-gather.3.cloned.1.call-start
  7.2 1.3 fusion.13
  8.5 5.1 psum.35
  13.6 1.9 fusion.14
  15.5 0.0 all-gather.3.cloned.1.call-update
  15.5 0.0 reduce-scatter.5.cloned.1.call-start
  15.6 69.0 %all-gather.3.cloned.1.call-done = bf16[1408,2048]{1,0:T(8,128)(2,1)} async-done(((bf16[88,2048]{1,0:T(8,128)(2,1)}), bf16[1408,2048]{1,0:T(8,128)(2,1)}) %all-gather.3.cloned.1.call-update) | async-done | bytes 5767184 | tf_op jit(solution)/shard_map/all_gather | solution.py:14
  84.6 9.9 fusion.5
  94.5 0.0 copy-start.2
  94.5 0.0 reduce-scatter.5.cloned.1.call-update
  94.5 0.0 copy-start.3
  94.6 0.0 reduce-scatter.3.cloned.1.call-start
  94.6 0.6 copy-done.2
  95.2 7.4 fusion.2
  102.7 0.0 copy-done
  102.7 0.0 copy-done.3
  102.7 9.2 fusion.9
  111.9 0.0 copy-start.1
  111.9 0.0 reduce-scatter.3.cloned.1.call-update
  111.9 0.0 all-gather.5.cloned.1.call-start
  112.0 0.6 copy-done.1
  112.6 0.1 dynamic-slice_subtract_fusion
  112.7 34.0 %reduce-scatter.5.cloned.1.call-done = f32[704,640]{1,0:T(8,128)} async-done(((f32[1408,640]{1,0:T(8,128)}), f32[704,640]{1,0:T(8,128)}) %reduce-scatter.5.cloned.1.call-update) | async-done | bytes 1802256 | tf_op jit(solution)/shard_map/reduce_scatter | solution.py:23
  146.7 1.7 reduce_max.9
  148.3 331.6 %pmax.7 = f32[704]{0:T(1024)S(1)} all-reduce(f32[704]{0:T(1024)S(1)} %reduce_max.9), channel_id=1, replica_groups=mesh['dp'=16,'vocab'=8,'tensor'=2] {'dp','vocab'}, use_global_device_ids=true, to_apply=%region_7.8 | all-reduce | flops 704 | bytes 5632 | tf_op jit(solution)/shard_map/pmax | solution.py:34
  480.0 0.0 reduce-scatter.3.cloned.1.call-done
  480.0 2.9 multiply_reduce_fusion.1
  482.9 644.7 %all-reduce = (f32[704]{0:T(1024)S(1)}, f32[704]{0:T(1024)S(1)}, f32[704]{0:T(1024)S(1)}) all-reduce(f32[704]{0:T(1024)S(1)} %get-tuple-element.5, f32[704]{0:T(1024)S(1)} %get-tuple-element.6, f32[704]{0:T(1024)S(1)} %get-tuple-element.4), channel_id=1, replica_groups=mesh['dp'=16,'vocab'=8,'tensor'=2] {'dp','vocab'}, use_global_device_ids=true, to_apply=%region_11.12 | all-reduce | flops 2112 | bytes 16896 | tf_op jit(solution)/shard_map/psum | solution.py:36
  1127.6 2.7 multiply_convert_fusion
  1130.4 0.0 all-gather.5.cloned.1.call-update
  1130.4 4.4 copy.8
  1134.8 21.6 %all-gather.5.cloned.1.call-done = bf16[1408,640]{1,0:T(8,128)(2,1)} async-done(((bf16[704,640]{1,0:T(8,128)(2,1)}), bf16[1408,640]{1,0:T(8,128)(2,1)}) %all-gather.5.cloned.1.call-update) | async-done | bytes 1802256 | tf_op jit(solution)/shard_map/all_gather | solution.py:45
  1156.4 10.9 multiply_reduce_fusion
  1167.3 5.9 copy.9
  1173.2 335.3 %psum.39 = f32[2048]{0:T(1024)} all-reduce(f32[2048]{0:T(1024)S(1)} %get-tuple-element.10), channel_id=1, replica_groups=mesh['dp'=16,'vocab'=8,'tensor'=2] {'dp','vocab'}, use_global_device_ids=true, to_apply=%region_13.14 | all-reduce | flops 2048 | bytes 16384 | tf_op jit(solution)/shard_map/psum | solution.py:50
  (2 shorter events, 0.0 us)
Async XLA Ops:
  7.2 95.5 %copy-start = (bf16[2048,640]{1,0:T(8,128)(2,1)S(1)}, bf16[2048,640]{1,0:T(8,128)(2,1)}, u32[]{:S(2)}) copy-start(bf16[2048,640]{1,0:T(8,128)(2,1)} %param.10) | copy-start | bytes 7864324
  7.2 77.4 %all-gather.3.cloned.1.call-start = ((), (), s32[]{:S(2)}) async-start(), calls=%async_computation.2 | async-start | bytes 6127616 | tf_op jit(solution)/shard_map/all_gather | solution.py:14
  15.5 131.2 %reduce-scatter.5.cloned.1.call-start = ((), (), s32[]{:S(2)}) async-start(), calls=%async_computation.4 | async-start | bytes 5406720 | tf_op jit(solution)/shard_map/reduce_scatter | solution.py:23
  94.5 0.7 copy-start.2
  94.5 8.1 copy-start.3
  94.6 385.4 %reduce-scatter.3.cloned.1.call-start = ((), (), s32[]{:S(2)}) async-start(), calls=%async_computation.3 | async-start | bytes 5406720 | tf_op jit(solution)/shard_map/reduce_scatter | solution.py:24
  111.9 0.7 copy-start.1
  111.9 1044.5 %all-gather.5.cloned.1.call-start = ((), (), s32[]{:S(2)}) async-start(), calls=%async_computation.5 | async-start | bytes 2703360 | tf_op jit(solution)/shard_map/all_gather | solution.py:45
Sparse Core Ops, SparseCore 0:
  15.6 68.9 all-gather.2
  94.7 51.9 reduce-scatter.4
  149.3 54.8 reduce-scatter.2
  1130.5 25.8 all-gather.4
where the time goes:
time: 1520 us
  blocking collectives  1320 us (87%)
  waiting for transfers between devices  125 us (8%)
  matrix products  37.5 us (2%)
    psum x1, blocking collectives, local(): lax.psum((jnp.sum(scaled_exp, axis=1), jnp.sum(scaled_exp * tangent_logit...  645 us
    psum x1, blocking collectives, local(): lax.psum(jnp.sum(head_weight.astype(jnp.float32) * product, axis=1), ('dp...  335 us
    pmax x1, blocking collectives, local(): row_top = lax.pmax(jnp.max(logits, axis=1), ('dp', 'vocab'))  332 us
    all_gather x1, waiting for transfers between devices, local(): gathered = lax.all_gather(normed, 'dp', axis=0, tiled=True)  69 us
    reduce_scatter x1, waiting for transfers between devices, local(): lax.psum_scatter(logits, 'tensor', scatter_dimension=0, tiled=True)  34 us
  transfers between devices with their start and end apart: 4, of which 3 were waited for; matrix products, arithmetic and copies ran while one was open for 2% of the time, Pallas kernels for 0%

commit v1 on v0

--- a/solution.py
+++ b/solution.py
@@ -47,8 +47,9 @@
         gathered, full_cot, (((0,), (0,)), ((), ())), preferred_element_type=jnp.float32
     )
     fisher_head = norm_gain[:, None] * product
-    fisher_gain = lax.psum(
-        jnp.sum(head_weight.astype(jnp.float32) * product, axis=1), ("dp", "vocab")
+    fisher_gain = jnp.sum(
+        lax.all_gather(jnp.sum(head_weight.astype(jnp.float32) * product, axis=1), ("dp", "vocab")),
+        axis=0,
     )
     return (fisher_head, fisher_gain)
 

time: 1520 us -> 1290 us (0.85)
  blocking collectives: 1320 us -> 981 us
  waiting for transfers between devices: 125 us -> 223 us
    psum x1 -> x0, blocking collectives: 335 us -> none  [local(): lax.psum(jnp.sum(head_weight.astype(jnp.float32) * product, axis=1), ('dp...]
    all_gather x0 -> x1, waiting for transfers between devices: none -> 98.7 us  [local(): lax.all_gather(jnp.sum(head_weight.astype(jnp.float32) * product, axis=1)...]
  transfers between devices with their start and end apart: 4 -> 5, of which waited for: 3 -> 4; matrix products, arithmetic and copies ran while one was open for 2% -> 2% of each run, Pallas kernels for 0% -> 0%
where the time goes in v1:
time: 1290 us; the launch traced here: 1280 us
  blocking collectives  981 us (76%)
  waiting for transfers between devices  223 us (17%)
  matrix products  38 us (3%)
  local copies, waits for them, and re-layouts  13.9 us (1%)
  between operations  13.9 us (1%)
    psum x1, blocking collectives, local(): lax.psum((jnp.sum(scaled_exp, axis=1), jnp.sum(scaled_exp * tangent_logit...  645 us
    pmax x1, blocking collectives, local(): row_top = lax.pmax(jnp.max(logits, axis=1), ('dp', 'vocab'))  332 us
    all_gather x1, waiting for transfers between devices, local(): lax.all_gather(jnp.sum(head_weight.astype(jnp.float32) * product, axis=1)...  98.7 us
    all_gather x1, waiting for transfers between devices, local(): gathered = lax.all_gather(normed, 'dp', axis=0, tiled=True)  69 us
    reduce_scatter x1, waiting for transfers between devices, local(): lax.psum_scatter(logits, 'tensor', scatter_dimension=0, tiled=True)  34 us
  transfers between devices with their start and end apart: 5, of which 4 were waited for; matrix products, arithmetic and copies ran while one was open for 2% of the time, Pallas kernels for 0%

profile of v1, /device:TPU:8, one launch (start us, length us, event | category | flops | bytes accessed | tf_op | source)
XLA Modules:
  0.0 1283.3 jit_solution(13389705201986357541)
XLA Ops:
  7.2 0.0 copy-start
  7.2 0.0 all-gather.5.cloned.1.call-start
  7.2 1.3 fusion.13
  8.5 5.1 psum.28
  13.6 1.9 fusion.14
  15.5 0.0 all-gather.5.cloned.1.call-update
  15.5 0.0 reduce-scatter.5.cloned.1.call-start
  15.6 69.0 %all-gather.5.cloned.1.call-done = bf16[1408,2048]{1,0:T(8,128)(2,1)} async-done(((bf16[88,2048]{1,0:T(8,128)(2,1)}), bf16[1408,2048]{1,0:T(8,128)(2,1)}) %all-gather.5.cloned.1.call-update) | async-done | bytes 5767184 | tf_op jit(solution)/shard_map/all_gather | solution.py:14
  84.6 9.9 fusion.5
  94.5 0.0 copy-start.2
  94.5 0.0 reduce-scatter.5.cloned.1.call-update
  94.5 0.0 copy-start.3
  94.6 0.0 reduce-scatter.3.cloned.1.call-start
  94.6 0.6 copy-done.2
  95.2 7.4 fusion.2
  102.7 0.0 copy-done
  102.7 0.0 copy-done.3
  102.7 9.2 fusion.9
  111.9 0.0 copy-start.1
  111.9 0.0 reduce-scatter.3.cloned.1.call-update
  111.9 0.0 all-gather.7.cloned.1.call-start
  112.0 0.6 copy-done.1
  112.6 0.1 dynamic-slice_subtract_fusion
  112.7 34.0 %reduce-scatter.5.cloned.1.call-done = f32[704,640]{1,0:T(8,128)} async-done(((f32[1408,640]{1,0:T(8,128)}), f32[704,640]{1,0:T(8,128)}) %reduce-scatter.5.cloned.1.call-update) | async-done | bytes 1802256 | tf_op jit(solution)/shard_map/reduce_scatter | solution.py:23
  146.7 1.7 reduce_max.9
  148.3 331.6 %pmax.7 = f32[704]{0:T(1024)S(1)} all-reduce(f32[704]{0:T(1024)S(1)} %reduce_max.9), channel_id=1, replica_groups=mesh['dp'=16,'vocab'=8,'tensor'=2] {'dp','vocab'}, use_global_device_ids=true, to_apply=%region_7.8 | all-reduce | flops 704 | bytes 5632 | tf_op jit(solution)/shard_map/pmax | solution.py:34
  480.0 0.0 reduce-scatter.3.cloned.1.call-done
  480.0 2.9 multiply_reduce_fusion.1
  482.9 644.7 %all-reduce = (f32[704]{0:T(1024)S(1)}, f32[704]{0:T(1024)S(1)}, f32[704]{0:T(1024)S(1)}) all-reduce(f32[704]{0:T(1024)S(1)} %get-tuple-element.9, f32[704]{0:T(1024)S(1)} %get-tuple-element.10, f32[704]{0:T(1024)S(1)} %get-tuple-element.8), channel_id=1, replica_groups=mesh['dp'=16,'vocab'=8,'tensor'=2] {'dp','vocab'}, use_global_device_ids=true, to_apply=%region_11.12 | all-reduce | flops 2112 | bytes 16896 | tf_op jit(solution)/shard_map/psum | solution.py:36
  1127.6 2.7 multiply_convert_fusion
  1130.4 0.0 all-gather.7.cloned.1.call-update
  1130.4 0.0 all-gather.9.cloned.1.call-start
  1130.4 4.4 copy.12
  1134.8 21.6 %all-gather.7.cloned.1.call-done = bf16[1408,640]{1,0:T(8,128)(2,1)} async-done(((bf16[704,640]{1,0:T(8,128)(2,1)}), bf16[1408,640]{1,0:T(8,128)(2,1)}) %all-gather.7.cloned.1.call-update) | async-done | bytes 1802256 | tf_op jit(solution)/shard_map/all_gather | solution.py:45
  1156.4 11.5 multiply_reduce_fusion
  1167.9 0.0 all-gather.9.cloned.1.call-update
  1167.9 5.9 copy.13
  1173.8 98.7 %all-gather.9.cloned.1.call-done = f32[262144]{0:T(1024)} async-done(((f32[2048]{0:T(1024)}), f32[262144]{0:T(1024)}) %all-gather.9.cloned.1.call-update) | async-done | bytes 1048592 | tf_op jit(solution)/shard_map/all_gather | solution.py:51
  1272.5 2.4 reshape.12
  1274.9 1.9 reduce_sum.59
  (2 shorter events, 0.0 us)
Async XLA Ops:
  7.2 95.5 %copy-start = (bf16[2048,640]{1,0:T(8,128)(2,1)S(1)}, bf16[2048,640]{1,0:T(8,128)(2,1)}, u32[]{:S(2)}) copy-start(bf16[2048,640]{1,0:T(8,128)(2,1)} %param.10) | copy-start | bytes 7864324
  7.2 77.4 %all-gather.5.cloned.1.call-start = ((), (), s32[]{:S(2)}) async-start(), calls=%async_computation.2 | async-start | bytes 6127616 | tf_op jit(solution)/shard_map/all_gather | solution.py:14
  15.5 131.2 %reduce-scatter.5.cloned.1.call-start = ((), (), s32[]{:S(2)}) async-start(), calls=%async_computation.4 | async-start | bytes 5406720 | tf_op jit(solution)/shard_map/reduce_scatter | solution.py:23
  94.5 0.7 copy-start.2
  94.5 8.1 copy-start.3
  94.6 385.4 %reduce-scatter.3.cloned.1.call-start = ((), (), s32[]{:S(2)}) async-start(), calls=%async_computation.3 | async-start | bytes 5406720 | tf_op jit(solution)/shard_map/reduce_scatter | solution.py:24
  111.9 0.7 copy-start.1
  111.9 1044.5 %all-gather.7.cloned.1.call-start = ((), (), s32[]{:S(2)}) async-start(), calls=%async_computation.5 | async-start | bytes 2703360 | tf_op jit(solution)/shard_map/all_gather | solution.py:45
  1130.4 142.1 %all-gather.9.cloned.1.call-start = ((), (), s32[]{:S(2)}) async-start(), calls=%async_computation.6 | async-start | bytes 1056768 | tf_op jit(solution)/shard_map/all_gather | solution.py:51
Sparse Core Ops, SparseCore 0:
  15.6 68.9 all-gather.4
  94.7 51.9 reduce-scatter.4
  149.3 54.8 reduce-scatter.2
  1130.5 25.8 all-gather.6
  1168.0 104.4 all-gather.8
